TPU v7x, 256 devices: a whole 4x4x8 slice. The times are simulated.
256 devices in a mesh: dp: 128 (over z, x, y), pair: 2 (over core).
Axes of the slice: x: 4, y: 4, z: 8, core: 2. Of those that a mesh axis runs over, the one named last changes fastest.
Arguments:
- embeddings: float32 [65536, 1024], P(('dp', 'pair')), may hold values from -140 to 140
- block_ids: int32 [128, 2, 512], replicated, may hold values from 0 to 65536, as said below
- block_counts: int32 [128], replicated, may hold values from 0 to 2, as said below
Outputs:
- max_similarity: float32 [65536], P(('dp', 'pair'))
Inputs may be any that keep to these rules, and one draw needn't show every extreme that they name: `block_ids`: every document stands in exactly one live slot of one cluster; slots past a cluster's block_counts and the tail of its last block hold 65536; each device gives exactly 4 documents to clusters 2 i and 2 i + 1 together, and at most 4 to one cluster; some cluster takes 4 documents from every device and fills its 2 blocks. `block_counts`: the number of blocks that a cluster's documents fill.
All inputs are finite; a program needn't handle non-finite values.
Results may differ from a plain program's by a relative error of at most 0.0018.
Values may be sent and summed in bfloat16 or wider, within the bound.
No kernel may reach another device: no remote copies, remote signals or barrier semaphores. Data moves between devices by JAX's collectives and lax.ppermute only.
A program may use at most 64 MiB of HBM per device.

v0:
```python
from functools import partial
import jax
import jax.numpy as jnp
from jax import lax
from jax.sharding import PartitionSpec as P


def keep_same(best_sim):
    return best_sim


def strip_scores(members, live_slots, block_rows, row_block, best_sim):
    start_row = row_block * block_rows
    rows_first = members[start_row : start_row + block_rows]
    columns = members[start_row:]
    live_first = live_slots[start_row : start_row + block_rows]
    live_columns = live_slots[start_row:]
    scores = jnp.dot(rows_first, columns.T, preferred_element_type=jnp.float32)
    same_cell = jnp.arange(block_rows)[:, None] == jnp.arange(columns.shape[0])[None, :]
    row_best = jnp.max(jnp.where(live_columns[None, :] & ~same_cell, scores, -1.0), axis=1)
    col_best = jnp.max(jnp.where(live_first[:, None] & ~same_cell, scores, -1.0), axis=0)
    best_sim = best_sim.at[start_row:].set(jnp.maximum(best_sim[start_row:], col_best))
    return best_sim.at[start_row : start_row + block_rows].set(
        jnp.maximum(best_sim[start_row : start_row + block_rows], row_best)
    )


def body(embeddings, block_ids, block_counts):
    doc_rows, feature = embeddings.shape
    chip_count = lax.axis_size("dp")
    my_chip = lax.axis_index("dp")
    my_core = lax.axis_index("pair")
    cluster_total, max_blocks, block_rows = block_ids.shape
    slot_total = max_blocks * block_rows
    doc_total = doc_rows * 2 * chip_count
    capacity = 2 * doc_rows // chip_count
    id_table = block_ids.reshape(cluster_total, slot_total)
    slot_index = jnp.arange(slot_total, dtype=jnp.int32)
    live_table = (slot_index[None, :] // block_rows < block_counts[:, None]) & (
        id_table < doc_total
    )
    square = jnp.sum(embeddings * embeddings, axis=1, keepdims=True)
    normed = (embeddings * lax.rsqrt(square + 1e-06)).astype(jnp.bfloat16)
    group_size = 1
    first_doc = (my_chip * 2 + my_core) * doc_rows
    group_span = group_size * doc_rows
    width_cap = group_size * capacity
    mine_slots = live_table & (id_table >= first_doc) & (id_table < first_doc + group_span)
    block_index = jnp.arange(block_rows, dtype=jnp.int32)
    strict_upper = (block_index[:, None] < block_index[None, :]).astype(jnp.bfloat16)
    mine_blocks = mine_slots.reshape(cluster_total * max_blocks, block_rows).astype(jnp.bfloat16)
    within_rank = jnp.dot(mine_blocks, strict_upper, preferred_element_type=jnp.float32).astype(
        jnp.int32
    )
    block_total = jnp.sum(
        mine_slots.reshape(cluster_total, max_blocks, block_rows).astype(jnp.int32), axis=2
    )
    block_before = jnp.cumsum(block_total, axis=1) - block_total
    send_rank = (
        within_rank.reshape(cluster_total, max_blocks, block_rows) + block_before[:, :, None]
    ).reshape(cluster_total, slot_total)
    rank_slot = jnp.arange(width_cap, dtype=jnp.int32)
    chosen = mine_slots[:, None, :] & (send_rank[:, None, :] == rank_slot[None, :, None])
    local_offset = (id_table - first_doc)[:, None, :]
    local_at = jnp.sum(jnp.where(chosen, local_offset, 0), axis=2) + jnp.where(
        jnp.any(chosen, axis=2), 0, group_span
    )
    doc_index = jnp.arange(group_span, dtype=jnp.int32)
    pick_docs = local_at.reshape(-1)[:, None] == doc_index[None, :]
    packed = jnp.dot(
        pick_docs.astype(jnp.bfloat16), normed, preferred_element_type=jnp.float32
    ).astype(jnp.bfloat16)
    packed = packed.reshape(cluster_total, width_cap, feature)
    received = lax.all_to_all(packed, "dp", split_axis=0, concat_axis=0, tiled=True)
    own_ids = lax.dynamic_index_in_dim(id_table, my_chip, 0, keepdims=False)
    own_live = lax.dynamic_index_in_dim(live_table, my_chip, 0, keepdims=False)
    live_blocks = lax.dynamic_index_in_dim(block_counts, my_chip, 0, keepdims=False)
    group_total = 2 * chip_count // group_size
    src_group = jnp.where(own_live, own_ids // group_span, group_total)
    earlier_same = (
        (src_group[:, None] == src_group[None, :])
        & own_live[None, :]
        & (slot_index[:, None] > slot_index[None, :])
    )
    own_rank = jnp.sum(earlier_same.astype(jnp.int32), axis=1)
    gathered = lax.all_gather(received, "pair", axis=0, tiled=True)
    row_pool = gathered.reshape(2 * chip_count * capacity, feature)
    dest_chip = src_group // 2
    source_core = src_group % 2
    pool_row = (source_core * chip_count + dest_chip) * capacity + own_rank
    accept_slot = own_live & (source_core == my_core)
    pool_row = jnp.where(own_live, pool_row, row_pool.shape[0])
    pool_index = jnp.arange(row_pool.shape[0], dtype=jnp.int32)
    pick_rows = (pool_row[:, None] == pool_index[None, :]).astype(jnp.bfloat16)
    members = jnp.dot(pick_rows, row_pool, preferred_element_type=jnp.float32).astype(jnp.bfloat16)
    best_sim = jnp.full((slot_total,), -1.0, jnp.float32)
    for row_block in range(max_blocks):
        taken = (row_block % 2 == my_core) & (row_block < live_blocks)
        best_sim = lax.cond(
            taken,
            partial(strip_scores, members, own_live, block_rows, row_block),
            keep_same,
            best_sim,
        )
    best_sim = lax.pmax(best_sim, "pair")
    target_slot = jnp.where(accept_slot, dest_chip * width_cap + own_rank, chip_count * width_cap)
    buffer_index = jnp.arange(chip_count * width_cap, dtype=jnp.int32)
    lands = target_slot[None, :] == buffer_index[:, None]
    back_buffer = jnp.max(jnp.where(lands, best_sim[None, :], -1.0), axis=1)
    returned = lax.all_to_all(
        back_buffer.reshape(chip_count, width_cap), "dp", split_axis=0, concat_axis=0, tiled=True
    )
    result = jnp.max(jnp.where(pick_docs, returned.reshape(-1)[:, None], -1.0), axis=0)
    return result


def solution(mesh):
    in_specs = (P(("dp", "pair"), None), P(), P())
    out_specs = P(("dp", "pair"))
    return jax.shard_map(body, mesh=mesh, in_specs=in_specs, out_specs=out_specs, check_vma=False)
```

profile of v0, /device:TPU:1, one launch (start us, length us, event | category | flops | bytes accessed | tf_op | source)
XLA Modules:
  0.0 124.0 jit_solution(2684171854075505043)
XLA Ops:
  6.5 0.0 copy-start.1
  6.5 0.0 all-gather.2.cloned.1.call-start
  6.6 1.4 %multiply_reduce_fusion = f32[256]{0:T(256)S(1)} fusion(f32[256,1024]{1,0:T(8,128)} %param.17), kind=kLoop, calls=%fused_computation.37 | loop fusion | flops 524032 | bytes 1049600 | tf_op jit(solution)/shard_map/reduce_sum | solution.py:42
  8.0 0.0 copy-start.2
  8.0 0.8 lt.113
  8.8 0.1 lt.114
  9.0 0.1 lt.111
  9.1 0.4 lt.112
  9.5 0.0 copy-done.1
  9.5 0.1 copy.7
  9.6 0.0 copy-done.2
  9.6 3.7 %fusion.17 = (s32[128,2]{1,0:T(8,128)S(1)}, pred[128,2,512]{2,1,0:T(4,128)(4,1)S(1)}, pred[128,2,512]{2,1,0:T(4,128)(4,1)S(1)}, pred[128,2,512]{2,1,0:T(4,128)(4,1)S(1)}) fusion(s32[2,512]{1,0:T(2,128)S(1)} %and_select_fusion.4, s32[128]{0:T(128)S(1)} %copy-done.2, s32[128,2,512]{2,1,0:T(2,128)S(1)} %copy-done.1, s32[]{:T(128)S(6)} %mul.39, s32[]{:T(128)S(6)} %add.116), kind=kLoop, calls=%fused_computation.43 | loop fusion | flops 1179392 | bytes 923144 | tf_op jit(solution)/shard_map/reduce_sum | solution.py:55
  13.4 0.3 compare_and_fusion
  13.6 0.3 lt.119
  14.0 0.2 reduce_window_sum.11
  14.2 0.3 ge.23
  14.5 0.3 lt.122
  14.8 0.4 convolution_convert_fusion.1
  15.2 0.2 reshape.352
  15.4 0.2 add.117
  15.6 0.0 copy-start
  15.6 0.1 copy.8
  15.7 0.1 add.119
  15.8 0.4 fusion.14
  16.2 0.5 select_reduce_fusion.5
  16.7 0.1 copy.5
  16.8 0.1 add.121
  16.9 0.0 copy-done
  16.9 0.5 convolution_convert_fusion
  17.4 0.4 reshape.353
  17.9 44.8 %all_to_all.14 = bf16[128,4,1024]{2,1,0:T(4,128)(2,1)} all-to-all(bf16[128,4,1024]{2,1,0:T(4,128)(2,1)S(1)} %reshape.353), channel_id=1, replica_groups=mesh['dp'=128,'pair'=2] {'dp'}, dimensions={0} | all-to-all | bytes 2097152 | tf_op jit(solution)/shard_map/all_to_all | solution.py:74
  62.7 0.0 all-gather.2.cloned.1.call-update
  62.8 0.6 dynamic_slice.14
  64.8 0.6 convert_reduce_fusion
  65.5 10.3 %all-gather.2.cloned.1.call-done = bf16[256,4,1024]{2,1,0:T(4,128)(2,1)} async-done(((bf16[128,4,1024]{2,1,0:T(4,128)(2,1)}), bf16[256,4,1024]{2,1,0:T(4,128)(2,1)}) %all-gather.2.cloned.1.call-update) | async-done | bytes 2097168 | tf_op jit(solution)/shard_map/all_gather | solution.py:86
  75.7 2.5 %reshape.354 = bf16[1024,1024]{1,0:T(8,128)(2,1)S(1)} reshape(bf16[256,4,1024]{2,1,0:T(4,128)(2,1)} %all-gather.2.cloned.1.call-done) | data formatting | bytes 4194304 | tf_op jit(solution)/shard_map/reshape | solution.py:87
  78.3 3.7 %fusion.15 = bf16[1024,1024]{1,0:T(8,128)(2,1)} fusion(bf16[1024,1024]{1,0:T(8,128)(2,1)S(1)} %reshape.354, s32[1024]{0:T(1024)S(1)} %fusion.30), kind=kOutput, calls=%fused_computation.33 | convolution fusion | flops 2149580800 | bytes 4198400 | tf_op jit(solution)/shard_map/dot_general | solution.py:95
  82.0 0.6 conditional.2
  82.0 0.6 broadcast_in_dim.55
  82.6 4.6 %conditional.3 = (f32[1024]{0:T(1024)}) conditional(s32[]{:T(128)} %convert_element_type.31, f32[1024]{0:T(1024)} %get-tuple-element.95, (f32[1024]{0:T(1024)}, pred[1024]{0:T(1024)(128)(4,1)S(1)}, bf16[1024,1024]{1,0:T(8,128)(2,1)}) %tuple.38), branch_computations={%region_10.11_spmd, %region_11.14_spmd} | conditional | flops 538968576 | bytes 1085448 | solution.py:99
  82.6 2.5 %select_reduce_fusion.2 = (f32[512]{0:T(512)S(1)}, f32[512]{0:T(512)S(1)}) fusion(pred[512]{0:T(512)(128)(4,1)S(1)} %slice.66, bf16[1024,1024]{1,0:T(8,128)(2,1)} %get-tuple-element.82), kind=kOutput, calls=%fused_computation.10 | convolution fusion | flops 538967040 | bytes 1053696 | tf_op jit(solution)/shard_map/cond/branch_1_fun/dot_general | solution.py:18
  85.2 0.7 copy.9
  85.9 0.7 maximum_dynamic-update-slice_fusion.1
  86.6 0.6 copy.15
  87.2 3.3 %pmax.7 = f32[1024]{0:T(1024)S(1)} all-reduce(f32[1024]{0:T(1024)} %get-tuple-element.96), channel_id=1, replica_groups=mesh['dp'=128,'pair'=2] {'pair'}, use_global_device_ids=true, to_apply=%region_14.15 | all-reduce | flops 1024 | bytes 8192 | tf_op jit(solution)/shard_map/pmax | solution.py:105
  90.4 0.3 select_reduce_fusion.4
  90.7 0.1 all_to_all.10
  90.8 24.1 %all_to_all.15 = f32[128,1,4]{2,1,0:T(1,128)S(1)} all-to-all(f32[128,1,4]{2,1,0:T(1,128)S(1)} %bitcast.21), channel_id=1, replica_groups=mesh['dp'=128,'pair'=2] {'dp'}, dimensions={0} | all-to-all | bytes 4096 | tf_op jit(solution)/shard_map/all_to_all | solution.py:110
  114.9 0.5 broadcast.371
  115.4 0.8 reduce.13
  116.3 0.1 broadcast_in_dim.106
  116.4 0.8 select_reduce_fusion.6
  (13 shorter events, 0.3 us)
Async XLA Ops:
  6.5 2.9 %copy-start.1 = (s32[128,2,512]{2,1,0:T(2,128)S(1)}, s32[128,2,512]{2,1,0:T(2,128)}, u32[]{:S(2)}) copy-start(s32[128,2,512]{2,1,0:T(2,128)} %param.18) | copy-start | bytes 1572868
  6.5 69.2 %all-gather.2.cloned.1.call-start = ((), (), s32[]{:S(2)}) async-start(), calls=%async_computation.2 | async-start | bytes 3145728 | tf_op jit(solution)/shard_map/all_gather | solution.py:86
  8.0 1.6 %copy-start.2 = (s32[128]{0:T(128)S(1)}, s32[128]{0:T(128)}, u32[]{:S(2)}) copy-start(s32[128]{0:T(128)} %param.19) | copy-start | bytes 1540
  15.6 1.3 %copy-start = (f32[256,1024]{1,0:T(8,128)S(1)}, f32[256,1024]{1,0:T(8,128)}, u32[]{:S(2)}) copy-start(f32[256,1024]{1,0:T(8,128)} %param.17) | copy-start | bytes 3145732
Sparse Core Ops, SparseCore 0:
  62.9 12.8 all-gather.1
where the time goes:
time: 124 us
  blocking collectives  72.2 us (58%)
  between operations  15 us (12%)
  waiting for transfers between devices  10.3 us (8%)
  other arithmetic  9.97 us (8%)
  local copies, waits for them, and re-layouts  9.37 us (8%)
  matrix products  7.18 us (6%)
    all_to_all x1, blocking collectives, body(): lax.all_to_all(packed, 'dp', split_axis=0, concat_axis=0, tiled=True)  44.8 us
    all_to_all x1, blocking collectives, body(): lax.all_to_all(back_buffer.reshape(chip_count, width_cap), 'dp', split_ax...  24.1 us
    all_gather x1, waiting for transfers between devices, body(): gathered = lax.all_gather(received, 'pair', axis=0, tiled=True)  10.3 us
    reduce_sum x1, other arithmetic, body(): jnp.sum(mine_slots.reshape(cluster_total, max_blocks, block_rows).astype(...  3.73 us
    dot_general x1, matrix products, body(): jnp.dot(pick_rows, row_pool, preferred_element_type=jnp.float32)  3.73 us
    pmax x1, blocking collectives, body(): best_sim = lax.pmax(best_sim, 'pair')  3.25 us
    dot_general x1, matrix products, strip_scores(): scores = jnp.dot(rows_first, columns.T, preferred_element_type=jnp.float32)  2.54 us
    reshape x1, local copies, waits for them, and re-layouts, body(): row_pool = gathered.reshape(2 * chip_count * capacity, feature)  2.54 us
  transfers between devices with their start and end apart: 1, of which 1 were waited for; matrix products, arithmetic and copies ran while one was open for 1% of the time, Pallas kernels for 0%

commit v1 on v0

--- a/solution.py
+++ b/solution.py
@@ -83,7 +83,9 @@
         & (slot_index[:, None] > slot_index[None, :])
     )
     own_rank = jnp.sum(earlier_same.astype(jnp.int32), axis=1)
-    gathered = lax.all_gather(received, "pair", axis=0, tiled=True)
+    gathered = jnp.concatenate(
+        lax.all_to_all(jnp.stack([received] * lax.axis_size("pair")), "pair", 0, 0), axis=0
+    )
     row_pool = gathered.reshape(2 * chip_count * capacity, feature)
     dest_chip = src_group // 2
     source_core = src_group % 2

time: 124 us -> 98.8 us (0.80)
  blocking collectives: 72.2 us -> 28.1 us
  starting transfers between devices: 0.01 us -> 16.3 us
  waiting for transfers between devices: 10.3 us -> 25.9 us
  between operations: 15 us -> 1.57 us
  matrix products: 7.18 us -> 5.75 us
    all_to_all x1, blocking collectives: 44.8 us -> 8.63 us  [body(): lax.all_to_all(jnp.stack([received] * lax.axis_size('pair')), 'pair', 0, 0)]
    all_to_all x0 -> x1, waiting for transfers between devices: none -> 25.9 us  [body(): lax.all_to_all(packed, 'dp', split_axis=0, concat_axis=0, tiled=True)]
    all_to_all x0 -> x1, starting transfers between devices: none -> 16.3 us  [body(): lax.all_to_all(packed, 'dp', split_axis=0, concat_axis=0, tiled=True)]
    all_gather x1 -> x0, waiting for transfers between devices: 10.3 us -> none  [body(): gathered = lax.all_gather(received, 'pair', axis=0, tiled=True)]
    all_to_all x1, blocking collectives: 24.1 us -> 16.4 us  [body(): lax.all_to_all(back_buffer.reshape(chip_count, width_cap), 'dp', split_ax...]
    reshape x1 -> x0, local copies, waits for them, and re-layouts: 2.54 us -> none  [body(): row_pool = gathered.reshape(2 * chip_count * capacity, feature)]
    another operation x0 -> x1, local copies, waits for them, and re-layouts: none -> 2.07 us  [body(): row_pool = gathered.reshape(2 * chip_count * capacity, feature)]
    dot_general x1, matrix products: 2.54 us -> 0.88 us  [strip_scores(): scores = jnp.dot(rows_first, columns.T, preferred_element_type=jnp.float32)]
where the time goes in v1:
time: 98.8 us; the launch traced here: 98.3 us
  blocking collectives  28.1 us (28%)
  waiting for transfers between devices  25.9 us (26%)
  starting transfers between devices  16.3 us (16%)
  other arithmetic  10.9 us (11%)
  local copies, waits for them, and re-layouts  9.7 us (10%)
  matrix products  5.75 us (6%)
  between operations  1.57 us (2%)
    all_to_all x1, waiting for transfers between devices, body(): lax.all_to_all(packed, 'dp', split_axis=0, concat_axis=0, tiled=True)  25.9 us
    all_to_all x1, blocking collectives, body(): lax.all_to_all(back_buffer.reshape(chip_count, width_cap), 'dp', split_ax...  16.4 us
    all_to_all x1, starting transfers between devices, body(): lax.all_to_all(packed, 'dp', split_axis=0, concat_axis=0, tiled=True)  16.3 us
    all_to_all x1, blocking collectives, body(): lax.all_to_all(jnp.stack([received] * lax.axis_size('pair')), 'pair', 0, 0)  8.63 us
    dot_general x1, matrix products, body(): jnp.dot(pick_rows, row_pool, preferred_element_type=jnp.float32)  3.96 us
    reduce_sum x1, other arithmetic, body(): jnp.sum(mine_slots.reshape(cluster_total, max_blocks, block_rows).astype(...  3.73 us
    pmax x1, blocking collectives, body(): best_sim = lax.pmax(best_sim, 'pair')  3.12 us
    another operation x1, local copies, waits for them, and re-layouts, body(): row_pool = gathered.reshape(2 * chip_count * capacity, feature)  2.07 us
  transfers between devices with their start and end apart: 1, of which 1 were waited for; matrix products, arithmetic and copies ran while one was open for 1% of the time, Pallas kernels for 0%

profile of v1, /device:TPU:1, one launch (start us, length us, event | category | flops | bytes accessed | tf_op | source)
XLA Modules:
  0.0 98.3 jit_solution(1701770429457501776)
XLA Ops:
  0.0 0.0 copy-start.1
  0.0 1.4 %multiply_reduce_fusion = f32[256]{0:T(256)S(1)} fusion(f32[256,1024]{1,0:T(8,128)} %param.17), kind=kLoop, calls=%fused_computation.38 | loop fusion | flops 524032 | bytes 1049600 | tf_op jit(solution)/shard_map/reduce_sum | solution.py:42
  1.5 0.0 copy-start.2
  1.5 0.8 lt.113
  2.3 0.1 lt.114
  2.4 0.1 lt.111
  2.6 0.4 lt.112
  2.9 0.0 copy-done.1
  2.9 0.1 copy.7
  3.1 0.0 copy-done.2
  3.1 3.7 %fusion.17 = (s32[128,2]{1,0:T(8,128)S(1)}, pred[128,2,512]{2,1,0:T(4,128)(4,1)S(1)}, pred[128,2,512]{2,1,0:T(4,128)(4,1)S(1)}, pred[128,2,512]{2,1,0:T(4,128)(4,1)S(1)}) fusion(s32[2,512]{1,0:T(2,128)S(1)} %and_select_fusion.4, s32[128]{0:T(128)S(1)} %copy-done.2, s32[128,2,512]{2,1,0:T(2,128)S(1)} %copy-done.1, s32[]{:T(128)S(6)} %mul.39, s32[]{:T(128)S(6)} %add.116), kind=kLoop, calls=%fused_computation.44 | loop fusion | flops 1179392 | bytes 923144 | tf_op jit(solution)/shard_map/reduce_sum | solution.py:55
  6.8 0.3 compare_and_fusion
  7.1 0.3 lt.119
  7.4 0.2 reduce_window_sum.11
  7.6 0.3 ge.23
  7.9 0.3 lt.122
  8.3 0.4 convolution_convert_fusion.1
  8.7 0.2 reshape.349
  8.8 0.2 add.117
  9.0 0.0 copy-start
  9.1 0.1 copy.8
  9.2 0.1 add.119
  9.2 0.4 fusion.14
  9.6 0.5 select_reduce_fusion.5
  10.2 0.1 copy.5
  10.3 0.1 add.121
  10.4 0.0 copy-done
  10.4 0.5 convolution_convert_fusion
  10.9 1.2 %reshape.350 = bf16[128,4,1024]{2,1,0:T(4,128)(2,1)} reshape(bf16[512,1024]{1,0:T(8,128)(2,1)S(1)} %convolution_convert_fusion) | data formatting | bytes 2097152 | tf_op jit(solution)/shard_map/reshape | solution.py:73
  12.1 16.3 %all-to-all-start = ((bf16[128,4,1024]{2,1,0:T(4,128)(2,1)}), bf16[128,4,1024]{2,1,0:T(4,128)(2,1)S(1)}, u32[]{:S(2)}, u32[]{:S(2)}) async-start(bf16[128,4,1024]{2,1,0:T(4,128)(2,1)} %reshape.350), calls=%async_computation | async-start | bytes 2097152 | tf_op jit(solution)/shard_map/all_to_all | solution.py:74
  28.5 0.6 dynamic_slice.14
  30.5 0.6 convert_reduce_fusion
  31.2 25.9 %all-to-all-done = bf16[128,4,1024]{2,1,0:T(4,128)(2,1)S(1)} async-done(((bf16[128,4,1024]{2,1,0:T(4,128)(2,1)}), bf16[128,4,1024]{2,1,0:T(4,128)(2,1)S(1)}, u32[]{:S(2)}, u32[]{:S(2)}) %all-to-all-start) | async-done | bytes 1048608 | tf_op jit(solution)/shard_map/all_to_all | solution.py:74
  57.1 1.0 pad_maximum_fusion
  58.0 8.6 %all_to_all.19 = bf16[2,128,4,1024]{3,2,1,0:T(4,128)(2,1)S(1)} all-to-all(bf16[2,128,4,1024]{3,2,1,0:T(4,128)(2,1)S(1)} %pad_maximum_fusion), channel_id=1, replica_groups=mesh['dp'=128,'pair'=2] {'pair'}, dimensions={0} | all-to-all | bytes 4194304 | tf_op jit(solution)/shard_map/all_to_all | solution.py:87
  66.7 2.1 %reshape_reshape.3 = bf16[1024,1024]{1,0:T(8,128)(2,1)} reshape(bf16[2,128,4,1024]{3,2,1,0:T(4,128)(2,1)S(1)} %all_to_all.19) | data formatting | bytes 4194304 | tf_op jit(solution)/shard_map/reshape;reshape | solution.py:89
  68.7 4.0 %fusion.15 = bf16[1024,1024]{1,0:T(8,128)(2,1)S(1)} fusion(bf16[1024,1024]{1,0:T(8,128)(2,1)} %reshape_reshape.3, s32[1024]{0:T(1024)S(1)} %fusion.30), kind=kOutput, calls=%fused_computation.34 | convolution fusion | flops 2149580800 | bytes 4198400 | tf_op jit(solution)/shard_map/dot_general | solution.py:97
  72.7 0.6 conditional.2
  72.7 0.6 broadcast_in_dim.55
  73.3 2.9 %conditional.3 = (f32[1024]{0:T(1024)}) conditional(s32[]{:T(128)} %convert_element_type.31, f32[1024]{0:T(1024)} %get-tuple-element.95, (f32[1024]{0:T(1024)}, pred[1024]{0:T(1024)(128)(4,1)S(1)}, bf16[1024,1024]{1,0:T(8,128)(2,1)S(1)}) %tuple.38), branch_computations={%region_10.11_spmd, %region_11.14_spmd} | conditional | flops 538968576 | bytes 1085448 | solution.py:101
  73.3 0.9 select_reduce_fusion.2
  74.2 0.7 copy.9
  74.9 0.7 maximum_dynamic-update-slice_fusion.1
  75.6 0.6 copy.15
  76.2 3.1 %pmax.7 = f32[1024]{0:T(1024)S(1)} all-reduce(f32[1024]{0:T(1024)} %get-tuple-element.96), channel_id=1, replica_groups=mesh['dp'=128,'pair'=2] {'pair'}, use_global_device_ids=true, to_apply=%region_14.15 | all-reduce | flops 1024 | bytes 8192 | tf_op jit(solution)/shard_map/pmax | solution.py:107
  79.3 0.3 select_reduce_fusion.4
  79.6 0.1 all_to_all.14
  79.7 16.4 %all_to_all.20 = f32[128,1,4]{2,1,0:T(1,128)S(1)} all-to-all(f32[128,1,4]{2,1,0:T(1,128)S(1)} %bitcast.23), channel_id=1, replica_groups=mesh['dp'=128,'pair'=2] {'dp'}, dimensions={0} | all-to-all | bytes 4096 | tf_op jit(solution)/shard_map/all_to_all | solution.py:112
  96.1 0.5 broadcast.371
  96.6 0.8 reduce.13
  97.5 0.1 broadcast_in_dim.106
  97.6 0.8 select_reduce_fusion.6
  (13 shorter events, 0.3 us)
Async XLA Ops:
  0.0 2.9 %copy-start.1 = (s32[128,2,512]{2,1,0:T(2,128)S(1)}, s32[128,2,512]{2,1,0:T(2,128)}, u32[]{:S(2)}) copy-start(s32[128,2,512]{2,1,0:T(2,128)} %param.18) | copy-start | bytes 1572868
  1.5 1.6 %copy-start.2 = (s32[128]{0:T(128)S(1)}, s32[128]{0:T(128)}, u32[]{:S(2)}) copy-start(s32[128]{0:T(128)} %param.19) | copy-start | bytes 1540
  9.0 1.3 %copy-start = (f32[256,1024]{1,0:T(8,128)S(1)}, f32[256,1024]{1,0:T(8,128)}, u32[]{:S(2)}) copy-start(f32[256,1024]{1,0:T(8,128)} %param.17) | copy-start | bytes 3145732
  12.1 44.9 %all-to-all-start = ((bf16[128,4,1024]{2,1,0:T(4,128)(2,1)}), bf16[128,4,1024]{2,1,0:T(4,128)(2,1)S(1)}, u32[]{:S(2)}, u32[]{:S(2)}) async-start(bf16[128,4,1024]{2,1,0:T(4,128)(2,1)} %reshape.350), calls=%async_computation | async-start | bytes 2097152 | tf_op jit(solution)/shard_map/all_to_all | solution.py:74
